TPU v7x, 512 devices: a whole 4x8x8 slice. The times are simulated.
512 devices in a mesh: leaf: 2 (over core), row: 8 (over y_hi, x), col: 32 (over y_lo, z).
Axes of the slice: x: 4, y: 8 (y_hi: 2, y_lo: 4; y = y_hi * 4 + y_lo), z: 8, core: 2. Of those that a mesh axis runs over, the one named last changes fastest.
Arguments:
- front: float32 [4096, 32768], P('row', ('leaf', 'col')), may hold values from -6 to 6
- child_update: float32 [2, 4096, 16384], P('leaf', ('row', 'col')), may hold values from -6 to 6
- block_pattern: int32 [2, 16, 64], replicated, may hold values 0 or 1
- child_map: int32 [2, 64], replicated, may hold values from 0 to 127, as said below
- block_slot: int32 [128], replicated, may hold values from 0 to 127, each once
- diag_inverse: float32 [2, 256, 256], replicated, as said below
Outputs:
- updated: float32 [4096, 32768], P('row', ('leaf', 'col'))
Inputs may be any that keep to these rules, and one draw needn't show every extreme that they name: `child_map`: each row lists 64 different parent blocks in increasing order and always includes blocks 0 and 127. `block_slot`: each slot once. `diag_inverse`: each matrix is lower triangular with a positive diagonal.
All inputs are finite; a program needn't handle non-finite values.
Results may differ from a plain program's by a relative error of at most 0.0001.
Values sent between devices are 32-bit elements; how exact they have to be, the bound alone decides.
A program may use at most 64 MiB of HBM per device.

v0:
```python
import jax
import jax.numpy as jnp
from jax import lax
from jax.sharding import PartitionSpec as P


def from_root(shard, axis, root):
    mine = lax.axis_index(axis) == root
    return lax.psum(jnp.where(mine, shard, jnp.zeros_like(shard)), axis)


def on_device(front, child_update, block_pattern, child_map, block_slot, diag_inverse):
    rows_dev, local_cols = front.shape
    block_size = diag_inverse.shape[1]
    sub_rows = child_update.shape[1]
    child_width = child_update.shape[2]
    child_blocks = child_width // block_size
    block_count = block_slot.shape[0]
    front_width = block_count * block_size
    leaf_count = lax.axis_size("leaf")
    col_count = lax.axis_size("col")
    leaf_id = lax.axis_index("leaf")
    row_id = lax.axis_index("row")
    col_id = lax.axis_index("col")
    global_rows = (row_id * col_count + col_id) * sub_rows + jnp.arange(sub_rows, dtype=jnp.int32)
    row_blocks = global_rows // block_size
    pattern_here = lax.dynamic_index_in_dim(block_pattern, leaf_id, 0, keepdims=False).astype(
        jnp.float32
    )
    onehot_rows = (
        row_blocks[:, None] == jnp.arange(block_pattern.shape[1], dtype=jnp.int32)[None, :]
    ).astype(jnp.float32)
    rows_present = jnp.dot(onehot_rows, pattern_here, precision=lax.Precision.HIGHEST)
    map_here = lax.dynamic_index_in_dim(child_map, leaf_id, 0, keepdims=False)
    parent_ids = jnp.arange(block_count, dtype=jnp.int32)
    target_slots = jnp.sum(
        jnp.where(map_here[:, None] == parent_ids[None, :], block_slot[None, :], 0), axis=1
    )
    pieces = child_update[0].reshape(sub_rows, child_blocks, block_size) * rows_present[:, :, None]
    extended = (
        jnp.zeros((sub_rows, block_count, block_size), jnp.float32)
        .at[:, target_slots, :]
        .set(pieces)
    )
    extended = extended.reshape(sub_rows, front_width)
    received = lax.all_to_all(extended, ("leaf", "col"), split_axis=1, concat_axis=0, tiled=True)
    working = front + jnp.sum(received.reshape(leaf_count, rows_dev, local_cols), axis=0)
    slots_local = local_cols // block_size
    owner_index = leaf_id * col_count + col_id
    my_slots = owner_index * slots_local + jnp.arange(slots_local, dtype=jnp.int32)
    slot_parent = jnp.sum(
        jnp.where(block_slot[None, :] == my_slots[:, None], parent_ids[None, :], 0), axis=1
    )
    local_rows = row_id * rows_dev + jnp.arange(rows_dev, dtype=jnp.int32)
    panel_count = diag_inverse.shape[0]
    for panel in range(panel_count):
        inverse = diag_inverse[panel]
        slot_here = block_slot[panel]
        owner_dev = slot_here // slots_local
        offset = slot_here % slots_local * block_size
        column = lax.dynamic_slice_in_dim(working, offset, block_size, 1)
        root_row = panel * block_size // rows_dev
        start_row = panel * block_size % rows_dev
        pivot_local = working[start_row : start_row + block_size]
        factored = from_root(
            jnp.dot(column, inverse.T, precision=lax.Precision.HIGHEST), ("leaf", "col"), owner_dev
        )
        pivot = from_root(
            jnp.dot(inverse, pivot_local, precision=lax.Precision.HIGHEST), "row", root_row
        )
        row_keep = local_rows >= (panel + 1) * block_size
        col_keep = jnp.repeat(slot_parent > panel, block_size)
        update_mask = row_keep[:, None] & col_keep[None, :]
        product = jnp.dot(factored, pivot, precision=lax.Precision.HIGHEST)
        working = working - jnp.where(update_mask, product, jnp.float32(0.0))
    return working


def solution(mesh):
    return jax.shard_map(
        on_device,
        mesh=mesh,
        in_specs=(P("row", ("leaf", "col")), P("leaf", ("row", "col"), None), P(), P(), P(), P()),
        out_specs=P("row", ("leaf", "col")),
        check_vma=False,
    )
```

profile of v0, /device:TPU:6, one launch (start us, length us, event | category | flops | bytes accessed | tf_op | source)
XLA Modules:
  0.0 1418.3 jit_solution(4548388972334492433)
XLA Ops:
  6.5 0.0 copy-start
  6.5 0.0 copy-start.4
  6.5 0.7 copy-done
  7.2 0.8 select_reduce_fusion
  8.1 1.5 copy.22
  9.6 0.0 copy-done.4
  9.6 0.2 fusion.17
  9.9 0.6 fusion.4
  10.5 0.2 broadcast_in_dim.50
  10.8 2.5 scatter_fusion
  13.3 2.6 copy.19
  15.9 1.9 all_to_all.12
  17.8 2.6 copy.20
  20.3 0.0 copy-start.3
  20.3 14.5 %all-to-all-start = ((f32[16,64,512]{2,0,1:T(8,128)}), f32[16,64,512]{2,0,1:T(8,128)S(1)}, u32[]{:S(2)}, u32[]{:S(2)}) async-start(f32[16,64,512]{2,0,1:T(8,128)} %copy.20), calls=%async_computation | async-start | bytes 4194304 | tf_op jit(solution)/shard_map/all_to_all | solution.py:46
  34.8 0.0 all-reduce.5.cloned.1.call-start
  34.9 0.0 copy-done.3
  34.9 0.6 fusion.30
  38.1 51.3 %all-to-all-done = f32[16,64,512]{2,0,1:T(8,128)S(1)} async-done(((f32[16,64,512]{2,0,1:T(8,128)}), f32[16,64,512]{2,0,1:T(8,128)S(1)}, u32[]{:S(2)}, u32[]{:S(2)}) %all-to-all-start) | async-done | bytes 2097184 | tf_op jit(solution)/shard_map/all_to_all | solution.py:46
  89.4 0.3 reduce_sum.31
  89.7 0.0 copy-start.1
  89.7 1.5 add.97
  91.3 0.0 copy-done.1
  91.3 1.4 convolution_select_fusion.5
  92.7 0.0 all-reduce.5.cloned.1.call-update
  92.7 0.0 all-reduce.7.cloned.1.call-start
  95.3 1.8 fusion.3
  97.1 0.0 copy-start.2
  97.1 0.0 all-reduce.7.cloned.1.call-update
  97.1 0.0 all-reduce.9.cloned.1.call-start
  97.2 0.2 fusion.24
  97.4 0.1 broadcast_in_dim.55
  97.5 545.2 %all-reduce.5.cloned.1.call-done = f32[512,256]{1,0:T(8,128)} async-done(((f32[512,256]{1,0:T(8,128)}), f32[512,256]{1,0:T(8,128)}) %all-reduce.5.cloned.1.call-update) | async-done | bytes 524304 | tf_op jit(solution)/shard_map/psum | solution.py:9
  642.6 110.2 %all-reduce.7.cloned.1.call-done = f32[256,512]{0,1:T(8,128)} async-done(((f32[256,512]{0,1:T(8,128)}), f32[256,512]{0,1:T(8,128)}) %all-reduce.7.cloned.1.call-update) | async-done | bytes 524304 | tf_op jit(solution)/shard_map/psum | solution.py:9
  752.9 2.3 fusion
  755.2 0.0 copy-done.2
  755.2 1.4 convolution_select_fusion.3
  756.6 0.0 all-reduce.9.cloned.1.call-update
  756.6 0.0 all-reduce.11.cloned.1.call-start
  756.7 1.8 fusion.2
  758.5 0.0 all-reduce.11.cloned.1.call-update
  758.5 0.1 broadcast_in_dim.57
  758.6 539.5 %all-reduce.9.cloned.1.call-done = f32[512,256]{1,0:T(8,128)} async-done(((f32[512,256]{1,0:T(8,128)}), f32[512,256]{1,0:T(8,128)}) %all-reduce.9.cloned.1.call-update) | async-done | bytes 524304 | tf_op jit(solution)/shard_map/psum | solution.py:9
  1298.1 110.3 %all-reduce.11.cloned.1.call-done = f32[256,512]{0,1:T(8,128)} async-done(((f32[256,512]{0,1:T(8,128)}), f32[256,512]{0,1:T(8,128)}) %all-reduce.11.cloned.1.call-update) | async-done | bytes 524304 | tf_op jit(solution)/shard_map/psum | solution.py:9
  1408.4 3.3 fusion.1
  (9 shorter events, 0.1 us)
Async XLA Ops:
  6.5 0.7 copy-start
  6.5 3.1 copy-start.4
  20.3 14.6 %copy-start.3 = (s32[128]{0:T(128)S(1)}, s32[128]{0:T(128)}, u32[]{:S(2)}) copy-start(s32[128]{0:T(128)} %param.10) | copy-start | bytes 1540
  20.3 69.1 %all-to-all-start = ((f32[16,64,512]{2,0,1:T(8,128)}), f32[16,64,512]{2,0,1:T(8,128)S(1)}, u32[]{:S(2)}, u32[]{:S(2)}) async-start(f32[16,64,512]{2,0,1:T(8,128)} %copy.20), calls=%async_computation | async-start | bytes 4194304 | tf_op jit(solution)/shard_map/all_to_all | solution.py:46
  34.8 607.8 %all-reduce.5.cloned.1.call-start = ((), (), s32[]{:S(2)}) async-start(), calls=%async_computation.1 | async-start | bytes 1048576 | tf_op jit(solution)/shard_map/psum | solution.py:9
  89.7 1.5 copy-start.1
  92.7 660.1 %all-reduce.7.cloned.1.call-start = ((), (), s32[]{:S(2)}) async-start(), calls=%async_computation.2 | async-start | bytes 1048576 | tf_op jit(solution)/shard_map/psum | solution.py:9
  97.1 658.1 %copy-start.2 = (f32[2,256,256]{2,1,0:T(8,128)S(1)}, f32[2,256,256]{2,1,0:T(8,128)}, u32[]{:S(2)}) copy-start(f32[2,256,256]{2,1,0:T(8,128)} %param.11) | copy-start | bytes 1572868
  97.1 1201.0 %all-reduce.9.cloned.1.call-start = ((), (), s32[]{:S(2)}) async-start(), calls=%async_computation.3 | async-start | bytes 1048576 | tf_op jit(solution)/shard_map/psum | solution.py:9
  756.6 651.8 %all-reduce.11.cloned.1.call-start = ((), (), s32[]{:S(2)}) async-start(), calls=%async_computation.4 | async-start | bytes 1048576 | tf_op jit(solution)/shard_map/psum | solution.py:9
Sparse Core Ops, SparseCore 0:
  92.8 549.7 all-reduce.4
  645.8 106.9 all-reduce.6
  756.8 541.3 all-reduce.8
  1301.1 107.2 all-reduce.10
where the time goes:
time: 1420 us
  waiting for transfers between devices  1360 us (96%)
  between operations  18.4 us (1%)
  starting transfers between devices  14.7 us (1%)
    psum x4, waiting for transfers between devices, from_root(): return lax.psum(jnp.where(mine, shard, jnp.zeros_like(shard)), axis)  1310 us
    all_to_all x1, waiting for transfers between devices, on_device(): lax.all_to_all(extended, ('leaf', 'col'), split_axis=1, concat_axis=0, ti...  51.3 us
  transfers between devices with their start and end apart: 5, of which 5 were waited for; matrix products, arithmetic and copies ran while one was open for 0% of the time, Pallas kernels for 0%

commit v1 on v0

v1 whole, which is shorter than its diff:
```python
import jax
import jax.numpy as jnp
from jax import lax
from jax.experimental import pallas as pl
from jax.experimental.pallas import tpu as pltpu
from jax.sharding import PartitionSpec as P

MESH = pl.DeviceIdType.MESH
F32 = jnp.float32
BF16 = jnp.bfloat16
NX = 4
NZ = 8


def split(v):
    hi = v.astype(BF16)
    return hi, (v - hi.astype(F32)).astype(BF16)


def dot3(a, b, trans=False):
    dims = (((1,), (1 if trans else 0,)), ((), ()))
    ah, al = split(a)
    bh, bl = split(b)

    def d(u, v):
        return lax.dot_general(u, v, dims, preferred_element_type=F32)

    return d(ah, bh) + (d(ah, bl) + d(al, bh))


def make_kernel(ncol, nrow, b, nb, cb_count, sub):
    ny = ncol // NZ
    crow = ncol * sub // ny
    half = nb // 2

    def kernel(
        child_h, front_h, w_h, tab_s, slot_v, out_h,
        childs, blocks, front, w, maskp, pairf, colsum, yrecv, ysum, zrecv,
        cb2, sendbuf, recv, work, rbuf, f0, f1, g, e, p0, p1,
        loc_sem, pair_s, pair_r, a2a_s, a2a_r, y_s, y_r, z_s, z_r, d_s, d_r,
        ya_s, ya_r, yd_s, yd_r, za_s, za_r, rs_s, rs_r, out_sem,
    ):
        leaf = lax.axis_index("leaf")
        row = lax.axis_index("row")
        col = lax.axis_index("col")
        y, z = col // NZ, lax.rem(col, NZ)
        x, yh = lax.rem(row, NX), row // NX
        other = 1 - leaf
        own = leaf * ncol + col

        def rcopy(src, dst, ssem, rsem, **dev):
            return pltpu.make_async_remote_copy(
                src_ref=src, dst_ref=dst, send_sem=ssem, recv_sem=rsem,
                device_id=dev, device_id_type=MESH,
            )

        barrier = pltpu.get_barrier_semaphore()
        pl.semaphore_signal(barrier, inc=1, device_id={"leaf": other}, device_id_type=MESH)

        @pl.loop(1, nrow)
        def _(k):
            pl.semaphore_signal(
                barrier, inc=1, device_id={"row": lax.rem(row + k, nrow)}, device_id_type=MESH
            )

        @pl.loop(1, ncol)
        def _(k):
            pl.semaphore_signal(
                barrier, inc=1, device_id={"col": lax.rem(col + k, ncol)}, device_id_type=MESH
            )

        front_cp = pltpu.make_async_copy(front_h, front, loc_sem.at[0])
        child_cp = pltpu.make_async_copy(child_h.at[0], childs.at[leaf], loc_sem.at[1])
        w_cp = pltpu.make_async_copy(w_h, w, loc_sem.at[2])
        front_cp.start()
        child_cp.start()
        w_cp.start()

        pl.semaphore_wait(barrier, 1 + (nrow - 1) + (ncol - 1))

        child_rc = rcopy(child_h.at[0], childs.at[leaf], pair_s.at[0], pair_r.at[0], leaf=other)
        child_rc.start()

        pivot_slot = [slot_v[:, q : q + 1] for q in range(2)]

        def held(panel, t):
            at = jnp.where(panel == 0, pivot_slot[0], pivot_slot[1])
            return jnp.where(at == 2 * own + t, 1.0, 0.0).astype(F32)

        def masked(panel, i):
            v = front[pl.ds(i * 4, 4)].reshape(4 * sub, 2 * b)
            return v[:, :b] * held(panel, 0) + v[:, b:] * held(panel, 1)

        front_cp.wait()

        @pl.loop(0, ncol // 4)
        def _(i):
            maskp[pl.ds(i * 4 * sub, 4 * sub), :] = masked(other, i)

        mask_rc = rcopy(maskp, pairf, pair_s.at[1], pair_r.at[1], leaf=other)
        mask_rc.start()
        mask_rc.wait_recv()

        @pl.loop(0, ncol // 4)
        def _(i):
            at = pl.ds(i * 4 * sub, 4 * sub)
            colsum[at, :] = masked(leaf, i) + pairf[at, :]

        def y_rs(dy):
            to = lax.rem(y + dy, ny)
            return rcopy(
                colsum.at[pl.ds(to * crow, crow)], yrecv.at[dy - 1], y_s.at[dy - 1], y_r.at[dy - 1],
                col=to * NZ + z,
            )

        for dy in range(1, ny):
            y_rs(dy).start()

        child_cp.wait()
        child_rc.wait_recv()

        @pl.loop(0, cb_count)
        def _(j):
            lanes = pl.ds(pl.multiple_of(j * b, b), b)
            for c in range(2):
                blocks[c * cb_count + j] = childs[c, :, lanes]

        def piece(r0, lane_at):
            total = None
            for c in range(2):
                at = tab_s[r0 + c, lane_at]
                v = blocks[c * cb_count + jnp.maximum(at - 1, 0)] * jnp.minimum(at, 1).astype(F32)
                total = v if total is None else total + v
            return total

        def a2a(k):
            to = lax.rem(col + k, ncol)
            return rcopy(sendbuf.at[k], recv.at[col], a2a_s.at[k], a2a_r.at[k], col=to)

        for t in range(2):
            recv[col, :, t * b : (t + 1) * b] = piece(0, leaf * half + 2 * col + t)

        @pl.loop(1, ncol)
        def _(k):
            to = lax.rem(col + k, ncol)
            for t in range(2):
                sendbuf[k, :, t * b : (t + 1) * b] = piece(0, leaf * half + 2 * to + t)
            a2a(k).start()

        for dy in range(1, ny):
            y_rs(dy).wait_recv()
        ysum[...] = colsum[pl.ds(y * crow, crow), :] + yrecv[0] + yrecv[1] + yrecv[2]

        def z_rs(dz):
            to = lax.rem(z + dz, NZ)
            return rcopy(
                ysum.at[pl.ds(to * sub, sub)], zrecv.at[dz - 1], z_s.at[dz - 1], z_r.at[dz - 1],
                col=y * NZ + to,
            )

        for dz in range(1, NZ):
            z_rs(dz).start()

        cross = lambda k: jnp.where(lax.rem(k, 3) == 2, 3, lax.rem(k, 3))

        def relays(k):
            q = lax.rem(k, 3)
            odd = lax.rem(k, 2) == 1
            src = lax.rem(col - k + ncol, ncol)

            def to(n, dst):
                return rcopy(rbuf.at[src], rbuf.at[src], rs_s.at[n, k], rs_r.at[k], row=dst)

            out = [
                (row == 0, to(0, 1)),
                (row == 0, to(1, 3)),
                ((row == 0) & (q == 0), to(2, NX)),
                (((row == 1) & odd) | ((row == 3) & ~odd), to(0, 2)),
                (((row == 1) & (q == 1)) | ((row == 3) & (q == 2)), to(1, row + NX)),
            ]
            for dx in range(1, NX):
                out.append(((yh == 1) & (x == cross(k)), to(dx - 1, NX + lax.rem(x + dx, NX))))
            return out

        def relay(k):
            src = lax.rem(col - k + ncol, ncol)

            @pl.when(row == 0)
            def _():
                @pl.when(k > 0)
                def _():
                    a2a(k).wait_recv()

                v = front[src] + recv[src]
                work[src] = v
                rbuf[src] = v

            @pl.when(row != 0)
            def _():
                rcopy(rbuf.at[src], rbuf.at[src], rs_s.at[0, k], rs_r.at[k], row=0 * row).wait_recv()

            for cond, cp in relays(k):
                pl.when(cond)(cp.start)

        def relay_range(lo, hi):
            @pl.loop(lo, hi)
            def _(k):
                relay(k)

        relay_range(0, 6)

        for dz in range(1, NZ):
            z_rs(dz).wait_recv()
        mine = ysum[pl.ds(z * sub, sub), :] + piece(2, leaf)
        for dz in range(1, NZ):
            mine = mine + zrecv[dz - 1]
        cb2[leaf, y, z] = mine

        has_d = (y // (ny // 2)) == other
        de = ny + lax.rem(y, ny // 2)

        def y_ag(dy):
            to = lax.rem(y + dy, ny)
            return rcopy(
                cb2.at[leaf, y, z], cb2.at[leaf, y, z], ya_s.at[dy - 1], ya_r.at[dy - 1],
                col=to * NZ + z,
            )

        for dy in range(1, ny):
            y_ag(dy).start()

        def d_send(k):
            return rcopy(
                cb2.at[leaf, y, z], cb2.at[leaf, de, z], d_s.at[k - 1], d_r, row=lax.rem(row + k, nrow)
            )

        @pl.when(has_d & (row == 0))
        def _():
            cb2[leaf, de, z] = mine
            for k in range(1, nrow):
                d_send(k).start()

        relay_range(6, 14)

        def y_dag(dy):
            to = lax.rem(y + dy, ny)
            return rcopy(
                cb2.at[leaf, de, z], cb2.at[leaf, de, z], yd_s.at[dy - 1], yd_r.at[dy - 1],
                col=to * NZ + z,
            )

        @pl.when(has_d)
        def _():
            @pl.when(row != 0)
            def _():
                d_send(1).wait_recv()

            for dy in range(1, ny):
                y_dag(dy).start()

        for dy in range(1, ny):
            y_ag(dy).wait_recv()

            @pl.when((lax.rem(y - dy + ny, ny) // (ny // 2)) == other)
            def _():
                y_dag(dy).wait_recv()

        def z_ag(dz):
            to = lax.rem(z + dz, NZ)
            return rcopy(
                cb2.at[leaf, :, z], cb2.at[leaf, :, z], za_s.at[dz - 1], za_r.at[dz - 1],
                col=y * NZ + to,
            )

        for dz in range(1, NZ):
            z_ag(dz).start()

        relay_range(14, 24)

        for dz in range(1, NZ):
            z_ag(dz).wait_recv()
        col_rc = rcopy(cb2.at[leaf], cb2.at[leaf], pair_s.at[2], pair_r.at[2], leaf=other)
        col_rc.start()
        w_cp.wait()
        col_rc.wait_recv()

        e[...] = dot3(w[0], cb2[1, ny : ny + ny // 2].reshape(b, b))

        @pl.loop(0, ny // 2)
        def _(i):
            g[pl.ds(i * crow, crow), :] = dot3(cb2[0, ny + i].reshape(crow, b), w[0], True)

        @pl.loop(0, ny)
        def _(i):
            at = pl.ds(i * crow, crow)
            fa = dot3(cb2[0, i].reshape(crow, b), w[0], True)
            c1 = cb2[1, i].reshape(crow, b) - dot3(fa, e[...])
            fb = dot3(c1, w[1], True)
            f0[at, :] = jnp.where((row > 0) | (i >= ny // 2), fa, 0.0)
            f1[at, :] = jnp.where(row > 0, fb, 0.0)

        relay_range(24, ncol)

        @pl.when(row != 0)
        def _():
            @pl.loop(0, ncol)
            def _(k):
                src = lax.rem(col - k + ncol, ncol)

                @pl.when(k > 0)
                def _():
                    a2a(k).wait_recv()

                work[src] = front[src] + recv[src]

        pr = b // sub

        def out_copy(i):
            at = pl.ds(i * NZ, NZ)
            return pltpu.make_async_copy(work.at[at], out_h.at[at], out_sem.at[i])

        for t in range(2):
            lanes = slice(t * b, (t + 1) * b)
            pa = dot3(w[0], rbuf[0:pr, :, lanes].reshape(b, b))
            zz = rbuf[pr : 2 * pr, :, lanes].reshape(b, b) - dot3(g[...], pa)
            p0[:, lanes] = pa
            p1[:, lanes] = dot3(w[1], zz)

        @pl.loop(0, ny)
        def _(i):
            at = pl.ds(i * crow, crow)
            for t in range(2):
                lanes = slice(t * b, (t + 1) * b)
                s = 2 * own + t
                k0 = jnp.broadcast_to(pivot_slot[0], (crow, b)) != s
                k1 = k0 & (jnp.broadcast_to(pivot_slot[1], (crow, b)) != s)
                v = work[pl.ds(i * NZ, NZ), :, lanes].reshape(crow, b)
                v = v - jnp.where(k0, dot3(f0[at, :], p0[:, lanes]), 0.0)
                v = v - jnp.where(k1, dot3(f1[at, :], p1[:, lanes]), 0.0)
                work[pl.ds(i * NZ, NZ), :, lanes] = v.reshape(NZ, sub, b)
            out_copy(i).start()

        child_rc.wait_send()
        mask_rc.wait_send()
        col_rc.wait_send()
        for dy in range(1, ny):
            y_rs(dy).wait_send()
            y_ag(dy).wait_send()
        for dz in range(1, NZ):
            z_rs(dz).wait_send()
            z_ag(dz).wait_send()

        @pl.when(has_d)
        def _():
            for dy in range(1, ny):
                y_dag(dy).wait_send()

            @pl.when(row == 0)
            def _():
                for k in range(1, nrow):
                    d_send(k).wait_send()

        @pl.loop(1, ncol)
        def _(k):
            a2a(k).wait_send()

        @pl.loop(0, ncol)
        def _(k):
            for cond, cp in relays(k):
                pl.when(cond)(cp.wait_send)

        @pl.loop(0, ny)
        def _(i):
            out_copy(i).wait()

    dma = pltpu.SemaphoreType.DMA
    width = 2 * b
    rows = ncol * sub
    scratch = [
        pltpu.VMEM((2, sub, cb_count * b), F32),
        pltpu.VMEM((2 * cb_count, sub, b), F32),
        pltpu.VMEM((ncol, sub, width), F32),
        pltpu.VMEM((2, b, b), F32),
        pltpu.VMEM((rows, b), F32),
        pltpu.VMEM((rows, b), F32),
        pltpu.VMEM((rows, b), F32),
        pltpu.VMEM((ny - 1, crow, b), F32),
        pltpu.VMEM((crow, b), F32),
        pltpu.VMEM((NZ - 1, sub, b), F32),
        pltpu.VMEM((2, ny + ny // 2, NZ, sub, b), F32),
        pltpu.VMEM((ncol, sub, width), F32),
        pltpu.VMEM((ncol, sub, width), F32),
        pltpu.VMEM((ncol, sub, width), F32),
        pltpu.VMEM((ncol, sub, width), F32),
        pltpu.VMEM((rows, b), F32),
        pltpu.VMEM((rows, b), F32),
        pltpu.VMEM((b, b), F32),
        pltpu.VMEM((b, b), F32),
        pltpu.VMEM((b, width), F32),
        pltpu.VMEM((b, width), F32),
        dma((4,)), dma((3,)), dma((3,)), dma((ncol,)), dma((ncol,)),
        dma((ny - 1,)), dma((ny - 1,)), dma((NZ - 1,)), dma((NZ - 1,)),
        dma((nrow - 1,)), dma,
        dma((ny - 1,)), dma((ny - 1,)), dma((ny - 1,)), dma((ny - 1,)),
        dma((NZ - 1,)), dma((NZ - 1,)), dma((3, ncol)), dma((ncol,)), dma((ny,)),
    ]
    return kernel, scratch


def on_device(front, child_update, block_pattern, child_map, block_slot, diag_inverse):
    rows, width = front.shape
    b = diag_inverse.shape[1]
    sub = child_update.shape[1]
    nb = block_slot.shape[0]
    cb_count = child_map.shape[1]
    ncol, nrow = lax.axis_size("col"), lax.axis_size("row")
    kernel, scratch = make_kernel(ncol, nrow, b, nb, cb_count, sub)
    row_block = (lax.axis_index("row") * ncol + lax.axis_index("col")) * sub // b
    present = lax.dynamic_index_in_dim(block_pattern, row_block, 1, keepdims=False)
    code = (present * (jnp.arange(cb_count, dtype=jnp.int32) + 1))[:, :, None]
    ids = jnp.arange(nb, dtype=jnp.int32)
    parents = child_map[:, :, None]
    slots = jnp.sum(jnp.where(parents == ids, block_slot, 0), axis=2, keepdims=True)
    tables = jnp.concatenate(
        [jnp.sum(jnp.where(key == ids, code, 0), axis=1) for key in (slots, parents)]
    )
    hbm = pl.BlockSpec(memory_space=pl.ANY)
    vmem = pl.BlockSpec(memory_space=pltpu.VMEM)
    out = pl.pallas_call(
        kernel,
        out_shape=jax.ShapeDtypeStruct((ncol, sub, width), F32),
        in_specs=[hbm, hbm, hbm, pl.BlockSpec(memory_space=pltpu.SMEM), vmem],
        out_specs=hbm,
        scratch_shapes=scratch,
        compiler_params=pltpu.CompilerParams(
            collective_id=0, has_side_effects=True, vmem_limit_bytes=40 << 20
        ),
        cost_estimate=pl.CostEstimate(
            flops=6 * 22 * b * b * b, bytes_accessed=12 * rows * width, transcendentals=0
        ),
    )(
        child_update, front.reshape(ncol, sub, width), diag_inverse,
        tables, block_slot.reshape(1, nb),
    )
    return out.reshape(rows, width)


def solution(mesh):
    return jax.shard_map(
        on_device,
        mesh=mesh,
        in_specs=(P("row", ("leaf", "col")), P("leaf", ("row", "col"), None), P(), P(), P(), P()),
        out_specs=P("row", ("leaf", "col")),
        check_vma=False,
    )
```

time: 1420 us -> 183 us (0.13)
  the two profiles are of different devices: /device:TPU:6 before, /device:TPU:40 now
where the time goes in v1:
time: 183 us
  Pallas kernels  177 us (97%)
  local copies, waits for them, and re-layouts  5.85 us (3%)
    pallas_call x1, Pallas kernels, on_device(): pl.pallas_call(kernel, out_shape=jax.ShapeDtypeStruct((ncol, sub, width),...  177 us
    unnamed x13, local copies, waits for them, and re-layouts  5.85 us

profile of v1, /device:TPU:40, one launch (start us, length us, event | category | flops | bytes accessed | tf_op | source)
XLA Modules:
  0.0 182.9 jit_solution(4288621767439711552)
XLA Ops:
  0.0 0.0 copy-start
  0.0 0.7 copy-done
  0.7 0.0 copy-start.1
  0.7 0.0 copy-start.5
  0.8 0.6 copy-done.1
  1.4 0.0 copy-done.5
  1.4 0.2 select_reduce_fusion.2
  1.6 0.1 select_reduce_fusion.1
  1.8 0.0 copy-start.2
  1.8 1.2 copy-done.2
  3.0 0.0 copy-start.3
  3.0 1.2 copy-done.3
  4.2 0.0 copy-start.4
  4.2 1.0 copy-done.4
  5.3 176.7 %shard_map.64 = f32[32,16,512]{2,1,0:T(8,128)S(1)} custom-call(f32[1,16,16384]{2,1,0:T(8,128)S(1)} %copy-done.2, f32[32,16,512]{2,1,0:T(8,128)S(1)} %bitcast.6, f32[2,256,256]{2,1,0:T(8,128)S(1)} %copy-done.4, s32[4,128]{1,0:T(4,128)S(1)} %pad_add_fusion.tab_s, s32[1,128]{1,0:T(1,128)S(1)} %bitcast.5), custom_call_target="tpu_custom_call" | custom-call | flops 2214592512 | bytes 3145728 | tf_op jit(solution)/shard_map/pallas_call | solution.py:429
  181.9 1.0 copy.8
  (4 shorter events, 0.0 us)
Async XLA Ops:
  0.0 0.7 copy-start
  0.7 0.7 copy-start.1
  0.7 0.7 copy-start.5
  1.8 1.2 copy-start.2
  3.0 1.2 copy-start.3
  4.2 1.0 copy-start.4

commit v2 on v1

v2 whole, which is shorter than its diff:
```python
import jax
import jax.numpy as jnp
from jax import lax
from jax.experimental import pallas as pl
from jax.experimental.pallas import tpu as pltpu
from jax.sharding import PartitionSpec as P

MESH = pl.DeviceIdType.MESH
F32 = jnp.float32
BF16 = jnp.bfloat16
NX = 4
NZ = 8
UNITS = 8
TREE = (0, 0, 0, 0, 0, 0, 1, 1, 0, 0)
CROSS = (2, 2, 1, 3, 1, 3, 0, 0, 1, 3)
FIRST = ((0,), (1,), (2, 3, 4), (8, 9), (5, 6, 7))
OTHER = ((), (), (0, 1, 2, 3), (8, 9), (4, 5, 6, 7))


def split(v):
    hi = v.astype(BF16)
    return hi, (v - hi.astype(F32)).astype(BF16)


def dot3(a, b, trans=False):
    dims = (((1,), (1 if trans else 0,)), ((), ()))
    ah, al = split(a)
    bh, bl = split(b)

    def d(u, v):
        return lax.dot_general(u, v, dims, preferred_element_type=F32)

    return d(ah, bh) + (d(ah, bl) + d(al, bh))


def make_kernel(ncol, nrow, b, nb, cb_count, sub):
    ny = ncol // NZ
    crow = ncol * sub // ny
    per = ncol // UNITS
    half = nb // 2

    def kernel(
        child_h, front_h, w_h, tab_s, slot_v, out_h,
        childs, blocks, front, w, maskp, pairf, colsum, ybig, ysum, zsmall, zbig, zsum, ysmall,
        cb2, dbuf, sendbuf, recv, work, rbuf, pivots, f0, f1, g, e, p0, p1,
        loc_sem, pair_s, pair_r, a2a_s, a2a_r, y_s, y_r, z_s, z_r,
        ya_s, ya_r, za_s, za_r, rs_s, rs_r, out_sem,
    ):
        leaf = lax.axis_index("leaf")
        row = lax.axis_index("row")
        col = lax.axis_index("col")
        y, z = col // NZ, lax.rem(col, NZ)
        other = 1 - leaf
        own = leaf * ncol + col

        def rcopy(src, dst, ssem, rsem, **dev):
            return pltpu.make_async_remote_copy(
                src_ref=src, dst_ref=dst, send_sem=ssem, recv_sem=rsem,
                device_id=dev, device_id_type=MESH,
            )

        barrier = pltpu.get_barrier_semaphore()
        pl.semaphore_signal(barrier, inc=1, device_id={"leaf": other}, device_id_type=MESH)

        @pl.loop(1, nrow)
        def _(k):
            pl.semaphore_signal(
                barrier, inc=1, device_id={"row": lax.rem(row + k, nrow)}, device_id_type=MESH
            )

        @pl.loop(1, ncol)
        def _(k):
            pl.semaphore_signal(
                barrier, inc=1, device_id={"col": lax.rem(col + k, ncol)}, device_id_type=MESH
            )

        front_cp = pltpu.make_async_copy(front_h, front, loc_sem.at[0])
        child_cp = pltpu.make_async_copy(child_h.at[0], childs.at[leaf], loc_sem.at[1])
        w_cp = pltpu.make_async_copy(w_h, w, loc_sem.at[2])
        front_cp.start()
        child_cp.start()
        w_cp.start()

        pivot_slot = [slot_v[:, q : q + 1] for q in range(2)]

        def held(panel, t):
            at = jnp.where(panel == 0, pivot_slot[0], pivot_slot[1])
            return jnp.where(at == 2 * own + t, 1.0, 0.0).astype(F32)

        def masked(panel, i):
            v = front[pl.ds(i * NZ, NZ)].reshape(crow, 2 * b)
            return (v[:, :b] * held(panel, 0) + v[:, b:] * held(panel, 1)).reshape(NZ, sub, b)

        front_cp.wait()

        @pl.loop(0, ny)
        def _(i):
            maskp[i] = masked(other, i)

        mask_rc = rcopy(maskp, pairf, pair_s.at[1], pair_r.at[1], leaf=other)
        child_rc = rcopy(child_h.at[0], childs.at[leaf], pair_s.at[0], pair_r.at[0], leaf=other)
        pl.semaphore_wait(barrier, 1 + (nrow - 1) + (ncol - 1))
        mask_rc.start()
        child_rc.start()
        mask_rc.wait_recv()

        @pl.loop(0, ny)
        def _(i):
            colsum[i] = masked(leaf, i) + pairf[i]

        def y_to(dy):
            return lax.rem(y + dy, ny)

        def z_to(dz):
            return lax.rem(z + dz, NZ)

        def over_y(src, dst, ssem, rsem):
            return [
                rcopy(src(y_to(d)), dst(d - 1), ssem.at[d - 1], rsem.at[d - 1], col=y_to(d) * NZ + z)
                for d in range(1, ny)
            ]

        def over_z(src, dst, ssem, rsem):
            return [
                rcopy(src(z_to(d)), dst(d - 1), ssem.at[d - 1], rsem.at[d - 1], col=y * NZ + z_to(d))
                for d in range(1, NZ)
            ]

        def column_steps(which):
            if which == 0:
                return (
                    lambda: over_y(lambda t: colsum.at[t], lambda i: ybig.at[i], y_s, y_r),
                    lambda: over_z(lambda t: ysum.at[t], lambda i: zsmall.at[i], z_s, z_r),
                    lambda: over_z(lambda t: cb2.at[0, y, z], lambda i: cb2.at[0, y, z], za_s, za_r),
                    lambda: over_y(lambda t: cb2.at[0, y], lambda i: cb2.at[0, y], ya_s, ya_r),
                )
            return (
                lambda: over_z(lambda t: colsum.at[:, t], lambda i: zbig.at[i], z_s, z_r),
                lambda: over_y(lambda t: zsum.at[t], lambda i: ysmall.at[i], y_s, y_r),
                lambda: over_y(lambda t: cb2.at[1, y, z], lambda i: cb2.at[1, y, z], ya_s, ya_r),
                lambda: over_z(lambda t: cb2.at[1, :, z], lambda i: cb2.at[1, :, z], za_s, za_r),
            )

        def each_leaf(f):
            for which in range(2):
                pl.when(leaf == which)(lambda which=which: f(which, column_steps(which)))

        def start(copies):
            for cp in copies:
                cp.start()

        def arrive(copies):
            for cp in copies:
                cp.wait_recv()

        @each_leaf
        def _(which, steps):
            start(steps[0]())

        child_cp.wait()
        child_rc.wait_recv()

        @pl.loop(0, cb_count)
        def _(j):
            lanes = pl.ds(pl.multiple_of(j * b, b), b)
            for c in range(2):
                blocks[c * cb_count + j] = childs[c, :, lanes]

        def piece(r0, lane_at):
            total = None
            for c in range(2):
                at = tab_s[r0 + c, lane_at]
                v = blocks[c * cb_count + jnp.maximum(at - 1, 0)] * jnp.minimum(at, 1).astype(F32)
                total = v if total is None else total + v
            return total

        def a2a(k):
            to = lax.rem(col + k, ncol)
            return rcopy(sendbuf.at[k], recv.at[k], a2a_s.at[k], a2a_r.at[k], col=to)

        def back(k):
            return lax.rem(col - k + ncol, ncol)

        for t in range(2):
            recv[0, :, t * b : (t + 1) * b] = piece(0, leaf * half + 2 * col + t)

        @pl.loop(1, ncol)
        def _(k):
            to = lax.rem(col + k, ncol)
            for t in range(2):
                sendbuf[k, :, t * b : (t + 1) * b] = piece(0, leaf * half + 2 * to + t)
            a2a(k).start()

        def edges(u):
            rise = u % 2 == 0
            if TREE[u]:
                out = [(0, 1), (0, 3), (1, 2) if rise else (3, 2)]
            else:
                out = [(0, 1), (1, 2), (2, 3)] if rise else [(0, 3), (3, 2), (2, 1)]
            at = CROSS[u]
            out.append((at, at + NX))
            return out + [(at + NX, (at + d) % NX + NX) for d in range(1, NX)]

        def unit_ref(u):
            if u < UNITS:
                return rbuf.at[pl.ds(u * per, per)]
            return dbuf.at[leaf, u - UNITS]

        def unit_sends(u, src):
            return [
                rcopy(unit_ref(u), unit_ref(u), rs_s.at[n, u], rs_r.at[u], row=dst)
                for n, dst in enumerate(d for s, d in edges(u) if s == src)
            ]

        def unit_wait(u):
            rcopy(unit_ref(u), unit_ref(u), rs_s.at[0, u], rs_r.at[u], row=row).wait_recv()

        def relay(u, rows_of):
            for src in sorted({s for s, _ in edges(u) if (s == 0) == rows_of}):

                @pl.when(row == src)
                def _():
                    if src:
                        unit_wait(u)
                    elif u < UNITS:

                        @pl.loop(u * per, (u + 1) * per)
                        def _(k):
                            if u:
                                a2a(k).wait_recv()
                            else:
                                pl.when(k > 0)(lambda: a2a(k).wait_recv())
                            v = front[back(k)] + recv[k]
                            work[back(k)] = v
                            rbuf[k] = v
                    else:
                        dbuf[leaf, u - UNITS] = cb2[leaf, other * (ny // 2) + u - UNITS]
                    start(unit_sends(u, src))

        def do_relays(name):
            for u in FIRST[name]:
                relay(u, True)
            for u in OTHER[name]:
                relay(u, False)

        @each_leaf
        def _(which, steps):
            arrive(steps[0]())
            if which == 0:
                ysum[...] = colsum[y] + ybig[0] + ybig[1] + ybig[2]
            else:
                total = colsum[:, z]
                for d in range(NZ - 1):
                    total = total + zbig[d]
                zsum[...] = total
            start(steps[1]())

        do_relays(0)

        @each_leaf
        def _(which, steps):
            arrive(steps[1]())
            part, small, n = (ysum[z], zsmall, NZ - 1) if which == 0 else (zsum[y], ysmall, ny - 1)
            part = part + piece(2, which)
            for d in range(n):
                part = part + small[d]
            cb2[which, y, z] = part
            start(steps[2]())

        do_relays(1)

        @each_leaf
        def _(which, steps):
            arrive(steps[2]())
            start(steps[3]())

        do_relays(2)

        @each_leaf
        def _(which, steps):
            arrive(steps[3]())

        col_rc = rcopy(cb2.at[leaf], cb2.at[leaf], pair_s.at[2], pair_r.at[2], leaf=other)
        col_rc.start()
        do_relays(3)

        def leaf_only(f):
            for u in range(UNITS, UNITS + 2):
                for r in range(1, 2 * NX):
                    if r not in {s for s, _ in edges(u)}:
                        pl.when(row == r)(lambda u=u: f(u))

        do_relays(4)
        leaf_only(unit_wait)
        d_rc = rcopy(dbuf.at[leaf], dbuf.at[leaf], pair_s.at[3], pair_r.at[3], leaf=other)
        d_rc.start()
        w_cp.wait()
        col_rc.wait_recv()
        d_rc.wait_recv()

        e[...] = dot3(w[0], dbuf[1].reshape(b, b))

        @pl.loop(0, ny // 2)
        def _(i):
            g[pl.ds(i * crow, crow), :] = dot3(dbuf[0, i].reshape(crow, b), w[0], True)

        @pl.loop(0, ny)
        def _(i):
            at = pl.ds(i * crow, crow)
            fa = dot3(cb2[0, i].reshape(crow, b), w[0], True)
            c1 = cb2[1, i].reshape(crow, b) - dot3(fa, e[...])
            fb = dot3(c1, w[1], True)
            f0[at, :] = jnp.where((row > 0) | (i >= ny // 2), fa, 0.0)
            f1[at, :] = jnp.where(row > 0, fb, 0.0)

        @pl.when(row != 0)
        def _():
            @pl.loop(0, ncol)
            def _(k):
                pl.when(k > 0)(lambda: a2a(k).wait_recv())
                work[back(k)] = front[back(k)] + recv[k]

        for u in range(UNITS):
            for r in range(1, 2 * NX):
                if r not in {s for s, _ in edges(u)}:
                    pl.when(row == r)(lambda u=u: unit_wait(u))

        @pl.loop(0, ncol)
        def _(k):
            pivots[back(k)] = rbuf[k]

        pr = b // sub

        def out_copy(i):
            at = pl.ds(i * NZ, NZ)
            return pltpu.make_async_copy(work.at[at], out_h.at[at], out_sem.at[i])

        for t in range(2):
            lanes = slice(t * b, (t + 1) * b)
            pa = dot3(w[0], pivots[0:pr, :, lanes].reshape(b, b))
            zz = pivots[pr : 2 * pr, :, lanes].reshape(b, b) - dot3(g[...], pa)
            p0[:, lanes] = pa
            p1[:, lanes] = dot3(w[1], zz)
        @pl.loop(0, ny)
        def _(i):
            at = pl.ds(i * crow, crow)
            for t in range(2):
                lanes = slice(t * b, (t + 1) * b)
                s = 2 * own + t
                k0 = jnp.broadcast_to(pivot_slot[0], (crow, b)) != s
                k1 = k0 & (jnp.broadcast_to(pivot_slot[1], (crow, b)) != s)
                v = work[pl.ds(i * NZ, NZ), :, lanes].reshape(crow, b)
                v = v - jnp.where(k0, dot3(f0[at, :], p0[:, lanes]), 0.0)
                v = v - jnp.where(k1, dot3(f1[at, :], p1[:, lanes]), 0.0)
                work[pl.ds(i * NZ, NZ), :, lanes] = v.reshape(NZ, sub, b)
            out_copy(i).start()

        for cp in (child_rc, mask_rc, col_rc, d_rc):
            cp.wait_send()

        @each_leaf
        def _(which, steps):
            for step in steps:
                for cp in step():
                    cp.wait_send()

        @pl.loop(1, ncol)
        def _(k):
            a2a(k).wait_send()

        for u in range(UNITS + 2):
            for src in sorted({s for s, _ in edges(u)}):

                @pl.when(row == src)
                def _():
                    for cp in unit_sends(u, src):
                        cp.wait_send()

        @pl.loop(0, ny)
        def _(i):
            out_copy(i).wait()

    dma = pltpu.SemaphoreType.DMA
    width = 2 * b
    rows = ncol * sub
    scratch = [
        pltpu.VMEM((2, sub, cb_count * b), F32),
        pltpu.VMEM((2 * cb_count, sub, b), F32),
        pltpu.VMEM((ncol, sub, width), F32),
        pltpu.VMEM((2, b, b), F32),
        pltpu.VMEM((ny, NZ, sub, b), F32),
        pltpu.VMEM((ny, NZ, sub, b), F32),
        pltpu.VMEM((ny, NZ, sub, b), F32),
        pltpu.VMEM((ny - 1, NZ, sub, b), F32),
        pltpu.VMEM((NZ, sub, b), F32),
        pltpu.VMEM((NZ - 1, sub, b), F32),
        pltpu.VMEM((NZ - 1, ny, sub, b), F32),
        pltpu.VMEM((ny, sub, b), F32),
        pltpu.VMEM((ny - 1, sub, b), F32),
        pltpu.VMEM((2, ny, NZ, sub, b), F32),
        pltpu.VMEM((2, ny // 2, NZ, sub, b), F32),
        pltpu.VMEM((ncol, sub, width), F32),
        pltpu.VMEM((ncol, sub, width), F32),
        pltpu.VMEM((ncol, sub, width), F32),
        pltpu.VMEM((ncol, sub, width), F32),
        pltpu.VMEM((ncol, sub, width), F32),
        pltpu.VMEM((rows, b), F32),
        pltpu.VMEM((rows, b), F32),
        pltpu.VMEM((b, b), F32),
        pltpu.VMEM((b, b), F32),
        pltpu.VMEM((b, width), F32),
        pltpu.VMEM((b, width), F32),
        dma((4,)), dma((4,)), dma((4,)), dma((ncol,)), dma((ncol,)),
        dma((ny - 1,)), dma((ny - 1,)), dma((NZ - 1,)), dma((NZ - 1,)),
        dma((ny - 1,)), dma((ny - 1,)), dma((NZ - 1,)), dma((NZ - 1,)),
        dma((3, UNITS + 2)), dma((UNITS + 2,)), dma((ny,)),
    ]
    return kernel, scratch


def on_device(front, child_update, block_pattern, child_map, block_slot, diag_inverse):
    rows, width = front.shape
    b = diag_inverse.shape[1]
    sub = child_update.shape[1]
    nb = block_slot.shape[0]
    cb_count = child_map.shape[1]
    ncol, nrow = lax.axis_size("col"), lax.axis_size("row")
    kernel, scratch = make_kernel(ncol, nrow, b, nb, cb_count, sub)
    row_block = (lax.axis_index("row") * ncol + lax.axis_index("col")) * sub // b
    present = lax.dynamic_index_in_dim(block_pattern, row_block, 1, keepdims=False)
    code = (present * (jnp.arange(cb_count, dtype=jnp.int32) + 1))[:, :, None]
    ids = jnp.arange(nb, dtype=jnp.int32)
    parents = child_map[:, :, None]
    slots = jnp.sum(jnp.where(parents == ids, block_slot, 0), axis=2, keepdims=True)
    tables = jnp.concatenate(
        [jnp.sum(jnp.where(key == ids, code, 0), axis=1) for key in (slots, parents)]
    )
    hbm = pl.BlockSpec(memory_space=pl.ANY)
    vmem = pl.BlockSpec(memory_space=pltpu.VMEM)
    out = pl.pallas_call(
        kernel,
        out_shape=jax.ShapeDtypeStruct((ncol, sub, width), F32),
        in_specs=[hbm, hbm, hbm, pl.BlockSpec(memory_space=pltpu.SMEM), vmem],
        out_specs=hbm,
        scratch_shapes=scratch,
        compiler_params=pltpu.CompilerParams(
            collective_id=0, has_side_effects=True, vmem_limit_bytes=60 << 20
        ),
        cost_estimate=pl.CostEstimate(
            flops=6 * 22 * b * b * b, bytes_accessed=12 * rows * width, transcendentals=0
        ),
    )(
        child_update, front.reshape(ncol, sub, width), diag_inverse,
        tables, block_slot.reshape(1, nb),
    )
    return out.reshape(rows, width)


def solution(mesh):
    return jax.shard_map(
        on_device,
        mesh=mesh,
        in_specs=(P("row", ("leaf", "col")), P("leaf", ("row", "col"), None), P(), P(), P(), P()),
        out_specs=P("row", ("leaf", "col")),
        check_vma=False,
    )
```

time: 183 us -> 106 us (0.58)
  the two profiles are of different devices: /device:TPU:40 before, /device:TPU:49 now
where the time goes in v2:
time: 106 us
  Pallas kernels  101 us (95%)
  local copies, waits for them, and re-layouts  3.64 us (3%)
    pallas_call x1, Pallas kernels, on_device(): pl.pallas_call(kernel, out_shape=jax.ShapeDtypeStruct((ncol, sub, width),...  101 us
    unnamed x7, local copies, waits for them, and re-layouts  3.64 us

profile of v2, /device:TPU:49, one launch (start us, length us, event | category | flops | bytes accessed | tf_op | source)
XLA Modules:
  0.0 106.1 jit_solution(1785938472598808039)
XLA Ops:
  0.0 0.0 copy-start
  0.0 0.7 copy-done
  0.7 0.0 copy-start.1
  0.7 0.0 copy-start.2
  0.8 0.6 copy-done.1
  1.4 0.0 copy-done.2
  1.4 0.2 select_reduce_fusion.2
  1.6 0.1 select_reduce_fusion.1
  1.7 0.6 pad_add_fusion.tab_s
  2.3 101.5 %shard_map.64 = f32[32,16,512]{2,1,0:T(8,128)} custom-call(f32[1,16,16384]{2,1,0:T(8,128)} %child_h.1, f32[32,16,512]{2,1,0:T(8,128)} %bitcast.7, f32[2,256,256]{2,1,0:T(8,128)} %w_h.1, s32[4,128]{1,0:T(4,128)} %pad_add_fusion.tab_s, s32[1,128]{1,0:T(1,128)} %bitcast.6), custom_call_target="tpu_custom_call" | custom-call | flops 2214592512 | bytes 3145728 | tf_op jit(solution)/shard_map/pallas_call | solution.py:440
  103.8 2.3 %copy.8 = f32[512,512]{1,0:T(8,128)} copy(f32[512,512]{1,0:T(8,128)} %bitcast.4) | data formatting | bytes 2097152
  (3 shorter events, 0.0 us)
Async XLA Ops:
  0.0 0.7 copy-start
  0.7 0.7 copy-start.1
  0.7 0.7 copy-start.2

commit v3 on v2

--- a/solution.py
+++ b/solution.py
@@ -10,11 +10,6 @@
 BF16 = jnp.bfloat16
 NX = 4
 NZ = 8
-UNITS = 8
-TREE = (0, 0, 0, 0, 0, 0, 1, 1, 0, 0)
-CROSS = (2, 2, 1, 3, 1, 3, 0, 0, 1, 3)
-FIRST = ((0,), (1,), (2, 3, 4), (8, 9), (5, 6, 7))
-OTHER = ((), (), (0, 1, 2, 3), (8, 9), (4, 5, 6, 7))
 
 
 def split(v):
@@ -36,15 +31,15 @@
 def make_kernel(ncol, nrow, b, nb, cb_count, sub):
     ny = ncol // NZ
     crow = ncol * sub // ny
-    per = ncol // UNITS
+    fold = ncol // NX
     half = nb // 2
 
     def kernel(
         child_h, front_h, w_h, tab_s, slot_v, out_h,
         childs, blocks, front, w, maskp, pairf, colsum, ybig, ysum, zsmall, zbig, zsum, ysmall,
-        cb2, dbuf, sendbuf, recv, work, rbuf, pivots, f0, f1, g, e, p0, p1,
+        cb2, dbuf, sendbuf, recv, work, stage, front_x, rq, pivots, f0, f1, g, e, p0, p1,
         loc_sem, pair_s, pair_r, a2a_s, a2a_r, y_s, y_r, z_s, z_r,
-        ya_s, ya_r, za_s, za_r, rs_s, rs_r, out_sem,
+        ya_s, ya_r, za_s, za_r, rs_s, rs_r, rf_s, rf_r, rl_s, rl_r, rq_s, rq_r, d_s, d_r, dg_s, dg_r, dh_s, dh_r, out_sem,
     ):
         leaf = lax.axis_index("leaf")
         row = lax.axis_index("row")
@@ -88,7 +83,7 @@
             return jnp.where(at == 2 * own + t, 1.0, 0.0).astype(F32)
 
         def masked(panel, i):
-            v = front[pl.ds(i * NZ, NZ)].reshape(crow, 2 * b)
+            v = front[pl.ds(i * (NZ // NX), NZ // NX)].reshape(crow, 2 * b)
             return (v[:, :b] * held(panel, 0) + v[:, b:] * held(panel, 1)).reshape(NZ, sub, b)
 
         front_cp.wait()
@@ -102,6 +97,13 @@
         pl.semaphore_wait(barrier, 1 + (nrow - 1) + (ncol - 1))
         mask_rc.start()
         child_rc.start()
+
+        def lot(k):
+            return lax.rem(col - k + ncol, NX)
+
+        def front_to(k):
+            return rcopy(front.at[:, lot(k)], front_x, rf_s.at[k - 1], rf_r, row=k)
+
         mask_rc.wait_recv()
 
         @pl.loop(0, ny)
@@ -174,74 +176,159 @@
                 total = v if total is None else total + v
             return total
 
+        def slot_of(k):
+            return lax.rem(k, NX) * fold + k // NX
+
         def a2a(k):
             to = lax.rem(col + k, ncol)
-            return rcopy(sendbuf.at[k], recv.at[k], a2a_s.at[k], a2a_r.at[k], col=to)
+            return rcopy(sendbuf.at[slot_of(k)], recv.at[k], a2a_s.at[k], a2a_r.at[k], col=to)
 
         def back(k):
             return lax.rem(col - k + ncol, ncol)
 
-        for t in range(2):
-            recv[0, :, t * b : (t + 1) * b] = piece(0, leaf * half + 2 * col + t)
-
-        @pl.loop(1, ncol)
-        def _(k):
+        def build(k):
             to = lax.rem(col + k, ncol)
             for t in range(2):
-                sendbuf[k, :, t * b : (t + 1) * b] = piece(0, leaf * half + 2 * to + t)
-            a2a(k).start()
-
-        def edges(u):
-            rise = u % 2 == 0
-            if TREE[u]:
-                out = [(0, 1), (0, 3), (1, 2) if rise else (3, 2)]
+                sendbuf[slot_of(k), :, t * b : (t + 1) * b] = piece(0, leaf * half + 2 * to + t)
+
+        def lot_to(k):
+            return rcopy(
+                sendbuf.at[pl.ds(k * fold, fold)], stage, rl_s.at[k - 1], rl_r, row=k
+            )
+
+        def quarter(j):
+            to = lax.rem(col + NX * j + row, ncol)
+            src = stage.at[j]
+            return rcopy(src, rq.at[col // NX], rq_s.at[j], rq_r.at[j], col=to)
+
+        @pl.when(row == 0)
+        def _():
+            for k in (2, 1, 3):
+
+                @pl.loop(0, fold)
+                def _(j):
+                    build(NX * j + k)
+
+                lot_to(k).start()
+
+            for k in (2, 1, 3):
+                front_to(k).start()
+
+            @pl.loop(0, fold)
+            def _(j):
+                build(NX * j)
+                stage[j] = sendbuf[j]
+                pl.when(j > 0)(lambda: quarter(j).start())
+
+            rq[col // NX] = sendbuf[0]
+
+        @pl.when(row != 0)
+        def _():
+            build(0)
+            recv[0] = sendbuf[0]
+
+            @pl.loop(1, ncol)
+            def _(k):
+                build(k)
+                a2a(k).start()
+
+        def pass_on():
+            @pl.when((row > 0) & (row < NX))
+            def _():
+                lot_to(1).wait_recv()
+
+                @pl.loop(0, fold)
+                def _(j):
+                    quarter(j).start()
+
+        def share(k, to):
+            n = lax.rem(to - k + 2 * NX, NX)
+            return rcopy(pivots.at[:, lot(k)], pivots.at[:, lot(k)], rs_s.at[n], rs_r.at[k], row=to)
+
+        def shares():
+            x = lax.rem(row, NX)
+            here = row - x
+            return [share(x, here + lax.rem(x + d, NX)) for d in (2, 1, 3)]
+
+        def cross():
+            return share(row, row + NX)
+
+        def gather_pivots():
+            @pl.when(row < NX)
+            def _():
+                pl.when(row > 0)(lambda: front_to(1).wait_recv())
+
+                @pl.loop(0, fold)
+                def _(j):
+                    pl.when((row > 0) | (j > 0))(lambda: quarter(j).wait_recv())
+
+                m = lot(row)
+
+                @pl.when(row == 0)
+                def _():
+                    pivots[:, m] = front[:, m] + rq[...]
+
+                @pl.when(row > 0)
+                def _():
+                    pivots[:, m] = front_x[...] + rq[...]
+
+                cross().start()
+                start(shares())
+
+        def fan_pivots():
+            @pl.when(row >= NX)
+            def _():
+                share(row - NX, row).wait_recv()
+                start(shares())
+
+        d_own = y // (ny // 2) == other
+        d_at = lax.rem(y, ny // 2)
+
+        def d_out(k):
+            ref = dbuf.at[leaf, d_at, z]
+            return rcopy(ref, ref, d_s.at[k - 1], d_r, row=lax.rem(row + k, nrow))
+
+        def d_first(which):
+            ref = dbuf.at[which, d_at, z]
+            return (over_y if which else over_z)(lambda t: ref, lambda i: ref, dg_s, dg_r)
+
+        def d_second(which):
+            ref = dbuf.at[1, :, z] if which else dbuf.at[0, d_at]
+            return (over_z if which else over_y)(lambda t: ref, lambda i: ref, dh_s, dh_r)
+
+        def d_slices(part):
+            @pl.when(d_own & (row == 0))
+            def _():
+                dbuf[leaf, d_at, z] = part
+                for k in range(1, nrow):
+                    d_out(k).start()
+
+        def d_spread(which):
+            @pl.when(d_own)
+            def _():
+                pl.when(row > 0)(lambda: d_out(1).wait_recv())
+                start(d_first(which))
+
+        def y_arrive(copies):
+            for d, cp in enumerate(copies, 1):
+                pl.when(lax.rem(y - d + ny, ny) // (ny // 2) == other)(cp.wait_recv)
+
+        def d_gather(which):
+            if which:
+                y_arrive(d_first(1))
+                start(d_second(1))
             else:
-                out = [(0, 1), (1, 2), (2, 3)] if rise else [(0, 3), (3, 2), (2, 1)]
-            at = CROSS[u]
-            out.append((at, at + NX))
-            return out + [(at + NX, (at + d) % NX + NX) for d in range(1, NX)]
-
-        def unit_ref(u):
-            if u < UNITS:
-                return rbuf.at[pl.ds(u * per, per)]
-            return dbuf.at[leaf, u - UNITS]
-
-        def unit_sends(u, src):
-            return [
-                rcopy(unit_ref(u), unit_ref(u), rs_s.at[n, u], rs_r.at[u], row=dst)
-                for n, dst in enumerate(d for s, d in edges(u) if s == src)
-            ]
-
-        def unit_wait(u):
-            rcopy(unit_ref(u), unit_ref(u), rs_s.at[0, u], rs_r.at[u], row=row).wait_recv()
-
-        def relay(u, rows_of):
-            for src in sorted({s for s, _ in edges(u) if (s == 0) == rows_of}):
-
-                @pl.when(row == src)
+
+                @pl.when(d_own)
                 def _():
-                    if src:
-                        unit_wait(u)
-                    elif u < UNITS:
-
-                        @pl.loop(u * per, (u + 1) * per)
-                        def _(k):
-                            if u:
-                                a2a(k).wait_recv()
-                            else:
-                                pl.when(k > 0)(lambda: a2a(k).wait_recv())
-                            v = front[back(k)] + recv[k]
-                            work[back(k)] = v
-                            rbuf[k] = v
-                    else:
-                        dbuf[leaf, u - UNITS] = cb2[leaf, other * (ny // 2) + u - UNITS]
-                    start(unit_sends(u, src))
-
-        def do_relays(name):
-            for u in FIRST[name]:
-                relay(u, True)
-            for u in OTHER[name]:
-                relay(u, False)
+                    arrive(d_first(0))
+                    start(d_second(0))
+
+        def d_finish(which):
+            if which:
+                arrive(d_second(1))
+            else:
+                y_arrive(d_second(0))
 
         @each_leaf
         def _(which, steps):
@@ -255,7 +342,7 @@
                 zsum[...] = total
             start(steps[1]())
 
-        do_relays(0)
+        pass_on()
 
         @each_leaf
         def _(which, steps):
@@ -265,33 +352,27 @@
             for d in range(n):
                 part = part + small[d]
             cb2[which, y, z] = part
+            d_slices(part)
             start(steps[2]())
-
-        do_relays(1)
+            d_spread(which)
+
+        gather_pivots()
 
         @each_leaf
         def _(which, steps):
             arrive(steps[2]())
             start(steps[3]())
-
-        do_relays(2)
+            d_gather(which)
+
+        fan_pivots()
 
         @each_leaf
         def _(which, steps):
             arrive(steps[3]())
+            d_finish(which)
 
         col_rc = rcopy(cb2.at[leaf], cb2.at[leaf], pair_s.at[2], pair_r.at[2], leaf=other)
         col_rc.start()
-        do_relays(3)
-
-        def leaf_only(f):
-            for u in range(UNITS, UNITS + 2):
-                for r in range(1, 2 * NX):
-                    if r not in {s for s, _ in edges(u)}:
-                        pl.when(row == r)(lambda u=u: f(u))
-
-        do_relays(4)
-        leaf_only(unit_wait)
         d_rc = rcopy(dbuf.at[leaf], dbuf.at[leaf], pair_s.at[3], pair_r.at[3], leaf=other)
         d_rc.start()
         w_cp.wait()
@@ -318,18 +399,19 @@
             @pl.loop(0, ncol)
             def _(k):
                 pl.when(k > 0)(lambda: a2a(k).wait_recv())
-                work[back(k)] = front[back(k)] + recv[k]
-
-        for u in range(UNITS):
-            for r in range(1, 2 * NX):
-                if r not in {s for s, _ in edges(u)}:
-                    pl.when(row == r)(lambda u=u: unit_wait(u))
-
-        @pl.loop(0, ncol)
-        def _(k):
-            pivots[back(k)] = rbuf[k]
-
-        pr = b // sub
+                at = back(k)
+                work[at] = front[at // NX, lax.rem(at, NX)] + recv[k]
+
+        for k in range(NX):
+            pl.when((row != k) & (row != k + NX))(lambda k=k: share(k, row).wait_recv())
+
+        @pl.when(row == 0)
+        def _():
+            @pl.loop(0, fold)
+            def _(i):
+                work[pl.ds(i * NX, NX)] = pivots[i]
+
+        pr = b // sub // NX
 
         def out_copy(i):
             at = pl.ds(i * NZ, NZ)
@@ -337,8 +419,8 @@
 
         for t in range(2):
             lanes = slice(t * b, (t + 1) * b)
-            pa = dot3(w[0], pivots[0:pr, :, lanes].reshape(b, b))
-            zz = pivots[pr : 2 * pr, :, lanes].reshape(b, b) - dot3(g[...], pa)
+            pa = dot3(w[0], pivots[0:pr, :, :, lanes].reshape(b, b))
+            zz = pivots[pr : 2 * pr, :, :, lanes].reshape(b, b) - dot3(g[...], pa)
             p0[:, lanes] = pa
             p1[:, lanes] = dot3(w[1], zz)
         @pl.loop(0, ny)
@@ -364,16 +446,49 @@
                 for cp in step():
                     cp.wait_send()
 
-        @pl.loop(1, ncol)
-        def _(k):
-            a2a(k).wait_send()
-
-        for u in range(UNITS + 2):
-            for src in sorted({s for s, _ in edges(u)}):
-
-                @pl.when(row == src)
+        @pl.when(row != 0)
+        def _():
+            @pl.loop(1, ncol)
+            def _(k):
+                a2a(k).wait_send()
+
+        @pl.when(row == 0)
+        def _():
+            for k in range(1, NX):
+                front_to(k).wait_send()
+                lot_to(k).wait_send()
+
+        @pl.when(row < NX)
+        def _():
+            @pl.loop(0, fold)
+            def _(j):
+                pl.when((row > 0) | (j > 0))(lambda: quarter(j).wait_send())
+
+            cross().wait_send()
+
+        for cp in shares():
+            cp.wait_send()
+
+        @pl.when(d_own & (row == 0))
+        def _():
+            for k in range(1, nrow):
+                d_out(k).wait_send()
+
+        @each_leaf
+        def _(which, steps):
+            @pl.when(d_own)
+            def _():
+                for cp in d_first(which):
+                    cp.wait_send()
+
+            if which:
+                for cp in d_second(1):
+                    cp.wait_send()
+            else:
+
+                @pl.when(d_own)
                 def _():
-                    for cp in unit_sends(u, src):
+                    for cp in d_second(0):
                         cp.wait_send()
 
         @pl.loop(0, ny)
@@ -386,7 +501,7 @@
     scratch = [
         pltpu.VMEM((2, sub, cb_count * b), F32),
         pltpu.VMEM((2 * cb_count, sub, b), F32),
-        pltpu.VMEM((ncol, sub, width), F32),
+        pltpu.VMEM((fold, NX, sub, width), F32),
         pltpu.VMEM((2, b, b), F32),
         pltpu.VMEM((ny, NZ, sub, b), F32),
         pltpu.VMEM((ny, NZ, sub, b), F32),
@@ -402,8 +517,10 @@
         pltpu.VMEM((ncol, sub, width), F32),
         pltpu.VMEM((ncol, sub, width), F32),
         pltpu.VMEM((ncol, sub, width), F32),
-        pltpu.VMEM((ncol, sub, width), F32),
-        pltpu.VMEM((ncol, sub, width), F32),
+        pltpu.VMEM((fold, sub, width), F32),
+        pltpu.VMEM((fold, sub, width), F32),
+        pltpu.VMEM((fold, sub, width), F32),
+        pltpu.VMEM((fold, NX, sub, width), F32),
         pltpu.VMEM((rows, b), F32),
         pltpu.VMEM((rows, b), F32),
         pltpu.VMEM((b, b), F32),
@@ -413,7 +530,9 @@
         dma((4,)), dma((4,)), dma((4,)), dma((ncol,)), dma((ncol,)),
         dma((ny - 1,)), dma((ny - 1,)), dma((NZ - 1,)), dma((NZ - 1,)),
         dma((ny - 1,)), dma((ny - 1,)), dma((NZ - 1,)), dma((NZ - 1,)),
-        dma((3, UNITS + 2)), dma((UNITS + 2,)), dma((ny,)),
+        dma((NX,)), dma((NX,)), dma((NX - 1,)), dma, dma((NX - 1,)), dma,
+        dma((fold,)), dma((fold,)), dma((nrow - 1,)), dma,
+        dma((NZ - 1,)), dma((NZ - 1,)), dma((NZ - 1,)), dma((NZ - 1,)), dma((ny,)),
     ]
     return kernel, scratch
 
@@ -450,7 +569,7 @@
             flops=6 * 22 * b * b * b, bytes_accessed=12 * rows * width, transcendentals=0
         ),
     )(
-        child_update, front.reshape(ncol, sub, width), diag_inverse,
+        child_update, front.reshape(ncol // NX, NX, sub, width), diag_inverse,
         tables, block_slot.reshape(1, nb),
     )
     return out.reshape(rows, width)

time: 106 us -> 100 us (0.943)
  the two profiles are of different devices: /device:TPU:49 before, /device:TPU:10 now
where the time goes in v3:
time: 100 us; the launch traced here: 99.8 us
  Pallas kernels  95.2 us (95%)
  local copies, waits for them, and re-layouts  3.64 us (4%)
    pallas_call x1, Pallas kernels, on_device(): pl.pallas_call(kernel, out_shape=jax.ShapeDtypeStruct((ncol, sub, width),...  95.2 us
    unnamed x7, local copies, waits for them, and re-layouts  3.64 us

profile of v3, /device:TPU:10, one launch (start us, length us, event | category | flops | bytes accessed | tf_op | source)
XLA Modules:
  0.0 99.8 jit_solution(4636127380366689274)
XLA Ops:
  0.0 0.0 copy-start
  0.0 0.7 copy-done
  0.7 0.0 copy-start.1
  0.7 0.0 copy-start.2
  0.8 0.6 copy-done.1
  1.4 0.0 copy-done.2
  1.4 0.2 select_reduce_fusion.2
  1.6 0.1 select_reduce_fusion.1
  1.7 0.6 pad_add_fusion.tab_s
  2.3 95.2 %shard_map.64 = f32[32,16,512]{2,1,0:T(8,128)} custom-call(f32[1,16,16384]{2,1,0:T(8,128)} %child_h.1, f32[8,4,16,512]{3,2,1,0:T(8,128)} %bitcast.7, f32[2,256,256]{2,1,0:T(8,128)} %w_h.1, s32[4,128]{1,0:T(4,128)} %pad_add_fusion.tab_s, s32[1,128]{1,0:T(1,128)} %bitcast.6), custom_call_target="tpu_custom_call" | custom-call | flops 2214592512 | bytes 3145728 | tf_op jit(solution)/shard_map/pallas_call | solution.py:559
  97.5 2.3 %copy.8 = f32[512,512]{1,0:T(8,128)} copy(f32[512,512]{1,0:T(8,128)} %bitcast.4) | data formatting | bytes 2097152
  (3 shorter events, 0.0 us)
Async XLA Ops:
  0.0 0.7 copy-start
  0.7 0.7 copy-start.1
  0.7 0.7 copy-start.2
